TPU v7x, 32 devices: a whole 2x2x4 slice. The times are simulated.
32 devices in a mesh: prow: 8 (over z, x), pcol: 4 (over y, core).
Axes of the slice: x: 2, y: 2, z: 4, core: 2. Of those that a mesh axis runs over, the one named last changes fastest.
Arguments:
- sigma_top: bfloat16 [8192, 8192], P('prow', 'pcol'), may hold values from -400 to 400, as said below
- panel_par: bfloat16 [8192, 1024], P('prow', 'pcol'), may hold values from -0.119628906 to 0.119628906
- panel_kid: bfloat16 [8192, 2048], P('prow', 'pcol'), may hold values from -0.119628906 to 0.119628906
- link_kid: bfloat16 [8, 256, 256], P('pcol'), may hold values from -0.23925781 to 0.23925781
- dinv_par: float32 [4, 256, 256], P('pcol'), may hold values from -6 to 6
- dinv_kid: float32 [8, 256, 256], P('pcol'), may hold values from -6 to 6
- mask_par: int32 [4, 32], P('pcol', 'prow'), may hold values 0 or 1
- mask_kid: int32 [8, 32], P('pcol', 'prow'), may hold values 0 or 1
Outputs:
- sigma_par: bfloat16 [8192, 1024], P('prow', 'pcol')
- diag_par: float32 [4, 256, 256], P('pcol')
- sigma_kid: bfloat16 [8192, 2048], P('prow', 'pcol')
- link_sigma: float32 [8, 256, 256], P('pcol')
- diag_kid: float32 [8, 256, 256], P('pcol')
Inputs may be any that keep to these rules, and one draw needn't show every extreme that they name: `sigma_top`: symmetric.
All inputs are finite; a program needn't handle non-finite values. No bound on the sum of `mask_par` or of `mask_kid` on one device may be relied on, other than what follows from the above.
Results may differ from a plain program's by a relative error of at most 0.015.
Values may be sent and summed in bfloat16 or wider, within the bound.
A program may use at most 64 MiB of HBM per device.

v0:
```python
import jax
import jax.numpy as jnp
from jax import lax
from jax.sharding import PartitionSpec as P

KIDS = 2


def expand_rows(mask, width):
    count, blocks = mask.shape
    spread = jnp.broadcast_to(
        mask.T.astype(jnp.float32)[:, None, :, None], (blocks, width, count, width)
    )
    return spread.reshape(blocks * width, count * width)


def batch_mult(left, right):
    return jnp.einsum("cab,cbd->cad", left, right, precision=lax.Precision.HIGHEST)


def batch_tmult(left, right):
    return jnp.einsum("cba,cbd->cad", left, right, precision=lax.Precision.HIGHEST)


def on_device(sigma_top, panel_par, panel_kid, link_kid, dinv_par, dinv_kid, mask_par, mask_kid):
    width = dinv_par.shape[1]
    par_here = dinv_par.shape[0]
    kid_here = dinv_kid.shape[0]
    row_count = sigma_top.shape[0]
    kid_pattern = mask_kid * jnp.repeat(mask_par, KIDS, axis=0)
    par_rows = expand_rows(mask_par, width)
    kid_rows = expand_rows(kid_pattern, width)
    low_par = panel_par * par_rows.astype(jnp.bfloat16)
    low_kid = panel_kid * kid_rows.astype(jnp.bfloat16)
    sigma_rows = lax.all_gather(sigma_top, "pcol", axis=1, tiled=True)
    prod_par = jnp.dot(
        sigma_rows,
        lax.all_gather(low_par, "prow", axis=0, tiled=True),
        preferred_element_type=jnp.float32,
    )
    prod_kid = jnp.dot(
        sigma_rows,
        lax.all_gather(low_kid, "prow", axis=0, tiled=True),
        preferred_element_type=jnp.float32,
    )
    sigma_par = (-prod_par * par_rows).astype(jnp.bfloat16)
    par_blocks = sigma_par.reshape(row_count, par_here, width)
    par_spread = jnp.repeat(par_blocks, KIDS, axis=1)
    carried = jnp.einsum("rcb,cbd->rcd", par_spread, link_kid, preferred_element_type=jnp.float32)
    sigma_kid = (-(prod_kid + carried.reshape(row_count, kid_here * width)) * kid_rows).astype(
        jnp.bfloat16
    )
    low_par3 = low_par.reshape(row_count, par_here, width)
    low_kid3 = low_kid.reshape(row_count, kid_here, width)
    kid_blocks = sigma_kid.reshape(row_count, kid_here, width)
    part_par = jnp.einsum("rpb,rpd->pbd", low_par3, par_blocks, preferred_element_type=jnp.float32)
    part_cross = jnp.einsum(
        "rcb,rcd->cbd", par_spread, low_kid3, preferred_element_type=jnp.float32
    )
    part_kid = jnp.einsum("rcb,rcd->cbd", low_kid3, kid_blocks, preferred_element_type=jnp.float32)
    link_wide = link_kid.astype(jnp.float32)
    sum_par = lax.psum(part_par.astype(jnp.bfloat16), "prow").astype(jnp.float32)
    diag_par = dinv_par - sum_par
    diag_spread = jnp.repeat(diag_par, KIDS, axis=0)
    cross_sum, kid_sum = (
        lax.psum(part_cross.astype(jnp.bfloat16), "prow").astype(jnp.float32),
        lax.psum(part_kid.astype(jnp.bfloat16), "prow").astype(jnp.float32),
    )
    link_sigma = -(cross_sum + batch_mult(diag_spread, link_wide))
    diag_kid = dinv_kid - kid_sum - batch_tmult(link_wide, link_sigma)
    return (sigma_par, diag_par, sigma_kid, link_sigma, diag_kid)


def solution(mesh):
    placed = (
        P("prow", "pcol"),
        P("prow", "pcol"),
        P("prow", "pcol"),
        P("pcol", None, None),
        P("pcol", None, None),
        P("pcol", None, None),
        P("pcol", "prow"),
        P("pcol", "prow"),
    )
    return jax.shard_map(
        on_device,
        mesh=mesh,
        in_specs=placed,
        out_specs=(
            P("prow", "pcol"),
            P("pcol", None, None),
            P("prow", "pcol"),
            P("pcol", None, None),
            P("pcol", None, None),
        ),
        check_vma=False,
    )
```

profile of v0, /device:TPU:0, one launch (start us, length us, event | category | flops | bytes accessed | tf_op | source)
XLA Modules:
  0.0 421.5 jit_solution(7698292222596817835)
XLA Ops:
  7.2 0.0 all-gather.4.cloned.1.call-start
  7.3 0.7 bitcast_convert_fusion
  8.0 0.1 broadcast_bitcast_fusion
  8.1 2.0 broadcast_multiply_fusion
  10.1 0.0 all-gather.4.cloned.1.call-update
  10.2 0.0 all-gather.6.cloned.1.call-start
  10.2 0.7 all-gather.6.cloned.1.call-update
  10.9 0.0 all-gather.8.cloned.1.call-start
  11.0 1.3 copy.13
  12.3 0.3 broadcast_in_dim.25
  12.6 0.5 copy.29
  13.1 0.4 copy-done.3
  13.5 1.2 convert_multiply_fusion
  14.7 0.0 all-gather.8.cloned.1.call-update
  14.8 0.0 all-reduce.3.cloned.1.call-start
  14.8 72.1 %all-gather.4.cloned.1.call-done = bf16[8192,256]{1,0:T(8,128)(2,1)} async-done(((bf16[1024,256]{1,0:T(8,128)(2,1)}), bf16[8192,256]{1,0:T(8,128)(2,1)}) %all-gather.4.cloned.1.call-update) | async-done | bytes 4194320 | tf_op jit(solution)/shard_map/all_gather | solution.py:38
  86.9 105.8 %all-gather.6.cloned.1.call-done = bf16[1024,8192]{1,0:T(8,128)(2,1)} async-done(((bf16[1024,2048]{1,0:T(8,128)(2,1)}), bf16[1024,8192]{1,0:T(8,128)(2,1)}) %all-gather.6.cloned.1.call-update) | async-done | bytes 16777232 | tf_op jit(solution)/shard_map/all_gather | solution.py:35
  192.7 11.6 %fusion.4 = bf16[256,1024]{1,0:T(8,128)(2,1)S(1)} fusion(bf16[8192,256]{1,0:T(8,128)(2,1)} %all-gather.4.cloned.1.call-done, bf16[1024,8192]{1,0:T(8,128)(2,1)} %all-gather.6.cloned.1.call-done, f32[1024]{0:T(1024)S(1)} %bitcast.58), kind=kOutput, calls=%fused_computation.6 | convolution fusion | flops 4295753728 | bytes 21499904 | tf_op jit(solution)/shard_map/dot_general | solution.py:36
  204.3 1.0 fusion.7
  205.3 2.4 convolution_convert_fusion.1
  207.7 1.9 fusion.9
  209.6 110.7 %all-gather.8.cloned.1.call-done = bf16[8192,512]{0,1:T(8,128)(2,1)} async-done(((bf16[1024,512]{0,1:T(8,128)(2,1)}), bf16[8192,512]{0,1:T(8,128)(2,1)}) %all-gather.8.cloned.1.call-update) | async-done | bytes 8388624 | tf_op jit(solution)/shard_map/all_gather | solution.py:43
  320.4 15.2 %fusion.2 = bf16[1024,512]{0,1:T(8,128)(2,1)S(1)} fusion(f32[1024,512]{0,1:T(8,128)S(1)} %bitcast.48, f32[2,1024,256]{1,2,0:T(8,128)} %fusion.9, bf16[8192,512]{0,1:T(8,128)(2,1)} %all-gather.8.cloned.1.call-done, bf16[1024,8192]{1,0:T(8,128)(2,1)} %all-gather.6.cloned.1.call-done), kind=kOutput, calls=%fused_computation.3 | convolution fusion | flops 8592031744 | bytes 30408704 | tf_op jit(solution)/shard_map/dot_general | solution.py:41
  335.7 1.0 copy-done.7
  336.6 1.2 convolution_convert_fusion
  337.8 0.0 all-reduce.3.cloned.1.call-update
  337.8 1.0 copy.20
  338.8 2.3 copy.21
  341.1 69.0 %all-reduce.3.cloned.1.call-done = (bf16[1,256,256]{2,1,0:T(8,128)(2,1)}, bf16[2,256,256]{2,1,0:T(8,128)(2,1)}, bf16[2,256,256]{2,1,0:T(8,128)(2,1)}) async-done(((bf16[1,256,256]{2,1,0:T(8,128)(2,1)}, bf16[2,256,256]{2,1,0:T(8,128)(2,1)}, bf16[2,256,256]{2,1,0:T(8,128)(2,1)}), (bf16[1,256,256]{2,1,0:T(8,128)(2,1)}, bf16[2,256,256]{2,1,0:T(8,128)(2,1)}, ...) | async-done | bytes 655376 | tf_op jit(solution)/shard_map/psum | solution.py:62
  410.1 0.9 convert_subtract_fusion
  411.1 1.5 fusion.6
  412.6 2.4 fusion.5
  (25 shorter events, 0.1 us)
Async XLA Ops:
  7.2 200.6 %copy-start = (bf16[2,256,256]{2,1,0:T(8,128)(2,1)S(1)}, bf16[2,256,256]{2,1,0:T(8,128)(2,1)}, u32[]{:S(2)}) copy-start(bf16[2,256,256]{2,1,0:T(8,128)(2,1)} %param.11) | copy-start | bytes 786436
  7.2 5.1 %copy-start.11 = (s32[1,4]{1,0:T(1,128)S(1)}, s32[1,4]{1,0:T(1,128)}, u32[]{:S(2)}) copy-start(s32[1,4]{1,0:T(1,128)} %param.14) | copy-start | bytes 52
  7.2 3.8 copy-start.6
  7.2 5.1 %copy-start.10 = (s32[2,4]{1,0:T(2,128)S(1)}, s32[2,4]{1,0:T(2,128)}, u32[]{:S(2)}) copy-start(s32[2,4]{1,0:T(2,128)} %param.15) | copy-start | bytes 100
  7.2 79.7 %all-gather.4.cloned.1.call-start = ((), (), s32[]{:S(2)}) async-start(), calls=%async_computation | async-start | bytes 4718592 | tf_op jit(solution)/shard_map/all_gather | solution.py:38
  10.2 182.5 %all-gather.6.cloned.1.call-start = ((), (), s32[]{:S(2)}) async-start(), calls=%async_computation.1 | async-start | bytes 20971520 | tf_op jit(solution)/shard_map/all_gather | solution.py:35
  10.9 309.5 %all-gather.8.cloned.1.call-start = ((), (), s32[]{:S(2)}) async-start(), calls=%async_computation.2 | async-start | bytes 9437184 | tf_op jit(solution)/shard_map/all_gather | solution.py:43
  12.3 1.2 copy-start.3
  14.7 189.5 %copy-start.1 = (bf16[1024,256]{1,0:T(8,128)(2,1)S(1)}, bf16[1024,256]{1,0:T(8,128)(2,1)}, u32[]{:S(2)}) copy-start(bf16[1024,256]{1,0:T(8,128)(2,1)} %broadcast_multiply_fusion) | copy-start | bytes 1572868
  14.8 395.4 %all-reduce.3.cloned.1.call-start = ((), (), s32[]{:S(2)}) async-start(), calls=%async_computation.3 | async-start | bytes 1310720 | tf_op jit(solution)/shard_map/psum | solution.py:62
  320.4 16.3 %copy-start.2 = (bf16[1024,512]{0,1:T(8,128)(2,1)S(1)}, bf16[1024,512]{0,1:T(8,128)(2,1)}, u32[]{:S(2)}) copy-start(bf16[1024,512]{0,1:T(8,128)(2,1)} %convert_multiply_fusion) | copy-start | bytes 3145732
  335.6 1.0 copy-start.7
  335.6 74.5 %copy-start.9 = (f32[1,256,256]{2,1,0:T(8,128)S(1)}, f32[1,256,256]{2,1,0:T(8,128)}, u32[]{:S(2)}) copy-start(f32[1,256,256]{2,1,0:T(8,128)} %param.12) | copy-start | bytes 786436
  335.6 76.9 %copy-start.8 = (f32[2,256,256]{2,1,0:T(8,128)S(1)}, f32[2,256,256]{2,1,0:T(8,128)}, u32[]{:S(2)}) copy-start(f32[2,256,256]{2,1,0:T(8,128)} %param.13) | copy-start | bytes 1572868
  411.1 3.9 copy-start.5
  412.5 2.4 copy-start.4
Sparse Core Ops, SparseCore 0:
  10.7 76.0 all-gather.3
  88.4 104.1 all-gather.5
  195.4 124.9 all-gather.7
  337.9 72.1 all-reduce.2
where the time goes:
time: 422 us
  waiting for transfers between devices  358 us (85%)
  matrix products  37.2 us (9%)
  between operations  13.9 us (3%)
  local copies, waits for them, and re-layouts  6.89 us (2%)
  other arithmetic  4.93 us (1%)
    all_gather x1, waiting for transfers between devices, on_device(): lax.all_gather(low_kid, 'prow', axis=0, tiled=True)  111 us
    all_gather x1, waiting for transfers between devices, on_device(): sigma_rows = lax.all_gather(sigma_top, 'pcol', axis=1, tiled=True)  106 us
    all_gather x1, waiting for transfers between devices, on_device(): lax.all_gather(low_par, 'prow', axis=0, tiled=True)  72.1 us
    psum x1, waiting for transfers between devices, on_device(): lax.psum(part_par.astype(jnp.bfloat16), 'prow').astype(jnp.float32)  69 us
    dot_general x1, matrix products, on_device(): jnp.dot(sigma_rows, lax.all_gather(low_kid, 'prow', axis=0, tiled=True),...  15.2 us
    dot_general x1, matrix products, on_device(): jnp.dot(sigma_rows, lax.all_gather(low_par, 'prow', axis=0, tiled=True),...  11.6 us
  transfers between devices with their start and end apart: 4, of which 4 were waited for; matrix products, arithmetic and copies ran while one was open for 6% of the time, Pallas kernels for 0%

commit v1 on v0

--- a/solution.py
+++ b/solution.py
@@ -4,6 +4,28 @@
 from jax.sharding import PartitionSpec as P
 
 KIDS = 2
+
+
+def in_order(tiles, dim):
+    shape = list(tiles.shape[1:])
+    shape[dim] *= tiles.shape[0]
+    return jnp.moveaxis(tiles, 0, dim).reshape(shape)
+
+
+def ring_gather(x, axis, dim):
+    size = lax.axis_size(axis)
+    pairs = [(i, (i + 1) % size) for i in range(size)]
+    back = [(b, a) for a, b in pairs]
+    lower, upper = ([], [])
+    for step in range(size - 1):
+        if step % 2 == 0:
+            lower.append(lax.ppermute(lower[-1] if lower else x, axis, pairs))
+        else:
+            upper.append(lax.ppermute(upper[-1] if upper else x, axis, back))
+    blocks = jnp.stack([*lower[::-1], x, *upper])
+    shift = lax.axis_index(axis) - len(lower)
+    blocks = blocks[(jnp.arange(size) - shift) % size]
+    return in_order(blocks, dim)
 
 
 def expand_rows(mask, width):
@@ -34,9 +56,7 @@
     low_kid = panel_kid * kid_rows.astype(jnp.bfloat16)
     sigma_rows = lax.all_gather(sigma_top, "pcol", axis=1, tiled=True)
     prod_par = jnp.dot(
-        sigma_rows,
-        lax.all_gather(low_par, "prow", axis=0, tiled=True),
-        preferred_element_type=jnp.float32,
+        sigma_rows, ring_gather(low_par, "prow", 0), preferred_element_type=jnp.float32
     )
     prod_kid = jnp.dot(
         sigma_rows,

time: 422 us -> 348 us (0.82)
  waiting for transfers between devices: 358 us -> 230 us
  starting transfers between devices: 0.16 us -> 38.7 us
  local copies, waits for them, and re-layouts: 6.89 us -> 23.3 us
    all_gather x1, waiting for transfers between devices: 106 us -> 0.01 us  [on_device(): sigma_rows = lax.all_gather(sigma_top, 'pcol', axis=1, tiled=True)]
    all_gather x1 -> x0, waiting for transfers between devices: 72.1 us -> none  [on_device(): lax.all_gather(low_par, 'prow', axis=0, tiled=True)]
    ppermute x0 -> x7, waiting for transfers between devices: none -> 49.6 us  [the longest x4 49.6 us: ring_gather(): lower.append(lax.ppermute(lower[-1] if lower else x, axis, pairs))]
    ppermute x0 -> x7, starting transfers between devices: none -> 38.6 us  [the longest x3 30.6 us: ring_gather(): upper.append(lax.ppermute(upper[-1] if upper else x, axis, back))]
    unnamed x30 -> x38, local copies, waits for them, and re-layouts: 6.55 us -> 17.1 us
    gather x0 -> x1, local copies, waits for them, and re-layouts: none -> 4.98 us  [ring_gather(): blocks = blocks[(jnp.arange(size) - shift) % size]]
  transfers between devices with their start and end apart: 4 -> 10, of which waited for: 4 -> 6; matrix products, arithmetic and copies ran while one was open for 6% -> 12% of each run, Pallas kernels for 0% -> 0%
where the time goes in v1:
time: 348 us; the launch traced here: 347 us
  waiting for transfers between devices  230 us (66%)
  starting transfers between devices  38.7 us (11%)
  matrix products  37.2 us (11%)
  local copies, waits for them, and re-layouts  23.3 us (7%)
  between operations  13.9 us (4%)
  other arithmetic  4.32 us (1%)
    all_gather x1, waiting for transfers between devices, on_device(): lax.all_gather(low_kid, 'prow', axis=0, tiled=True)  110 us
    psum x1, waiting for transfers between devices, on_device(): lax.psum(part_par.astype(jnp.bfloat16), 'prow').astype(jnp.float32)  69 us
    ppermute x4, waiting for transfers between devices, ring_gather(): lower.append(lax.ppermute(lower[-1] if lower else x, axis, pairs))  49.6 us
    ppermute x3, starting transfers between devices, ring_gather(): upper.append(lax.ppermute(upper[-1] if upper else x, axis, back))  30.6 us
    unnamed x38, local copies, waits for them, and re-layouts  17.1 us
    dot_general x1, matrix products, on_device(): jnp.dot(sigma_rows, lax.all_gather(low_kid, 'prow', axis=0, tiled=True),...  15.2 us
    dot_general x1, matrix products, on_device(): jnp.dot(sigma_rows, ring_gather(low_par, 'prow', 0), preferred_element_ty...  11.6 us
    ppermute x4, starting transfers between devices, ring_gather(): lower.append(lax.ppermute(lower[-1] if lower else x, axis, pairs))  8.06 us
  transfers between devices with their start and end apart: 10, of which 6 were waited for; matrix products, arithmetic and copies ran while one was open for 12% of the time, Pallas kernels for 0%

profile of v1, /device:TPU:0, one launch (start us, length us, event | category | flops | bytes accessed | tf_op | source)
XLA Modules:
  0.0 347.1 jit_solution(13108362830967558140)
XLA Ops:
  9.8 1.1 convert_multiply_fusion
  11.1 1.2 broadcast_multiply_fusion
  12.4 3.0 collective-permute-start
  15.4 15.0 %collective-permute-done = bf16[1024,256]{1,0:T(8,128)(2,1)S(1)} collective-permute-done((bf16[1024,256]{1,0:T(8,128)(2,1)S(1)}, bf16[1024,256]{1,0:T(8,128)(2,1)S(1)}, u32[]{:S(2)}, u32[]{:S(2)}) %collective-permute-start) | collective-permute-done | bytes 524320 | tf_op jit(solution)/shard_map/ppermute | solution.py:22
  30.3 4.7 %collective-permute-start.4 = (bf16[1024,256]{1,0:T(8,128)(2,1)S(1)}, bf16[1024,256]{1,0:T(8,128)(2,1)}, u32[]{:S(2)}, u32[]{:S(2)}) collective-permute-start(bf16[1024,256]{1,0:T(8,128)(2,1)S(1)} %broadcast_multiply_fusion), channel_id=1, source_target_pairs={{4,0},{8,4},{12,8},{16,12},{20,16},{24,20},{28,24},{0,28},{5,1},{9... | collective-permute-start | bytes 1572872 | tf_op jit(solution)/shard_map/ppermute | solution.py:24
  35.0 17.4 %collective-permute-done.1 = bf16[1024,256]{1,0:T(8,128)(2,1)S(1)} collective-permute-done((bf16[1024,256]{1,0:T(8,128)(2,1)S(1)}, bf16[1024,256]{1,0:T(8,128)(2,1)S(1)}, u32[]{:S(2)}, u32[]{:S(2)}) %collective-permute-start.1) | collective-permute-done | bytes 524320 | tf_op jit(solution)/shard_map/ppermute | solution.py:22
  52.5 2.5 collective-permute-start.2
  55.0 12.2 %collective-permute-start.5 = (bf16[1024,256]{1,0:T(8,128)(2,1)}, bf16[1024,256]{1,0:T(8,128)(2,1)}, u32[]{:S(2)}, u32[]{:S(2)}) collective-permute-start(bf16[1024,256]{1,0:T(8,128)(2,1)} %collective-permute-done.4), channel_id=1, source_target_pairs={{4,0},{8,4},{12,8},{16,12},{20,16},{24,20},{28,24},{0,28},{5,1},{9... | collective-permute-start | bytes 1572872 | tf_op jit(solution)/shard_map/ppermute | solution.py:24
  67.2 9.3 %collective-permute-done.2 = bf16[1024,256]{1,0:T(8,128)(2,1)} collective-permute-done((bf16[1024,256]{1,0:T(8,128)(2,1)S(1)}, bf16[1024,256]{1,0:T(8,128)(2,1)}, u32[]{:S(2)}, u32[]{:S(2)}) %collective-permute-start.2) | collective-permute-done | bytes 524320 | tf_op jit(solution)/shard_map/ppermute | solution.py:22
  76.4 2.6 collective-permute-start.3
  79.0 13.6 %collective-permute-start.6 = (bf16[1024,256]{1,0:T(8,128)(2,1)}, bf16[1024,256]{1,0:T(8,128)(2,1)S(1)}, u32[]{:S(2)}, u32[]{:S(2)}) collective-permute-start(bf16[1024,256]{1,0:T(8,128)(2,1)} %collective-permute-done.5), channel_id=1, source_target_pairs={{4,0},{8,4},{12,8},{16,12},{20,16},{24,20},{28,24},{0,28},{5,1},{9... | collective-permute-start | bytes 1572872 | tf_op jit(solution)/shard_map/ppermute | solution.py:24
  92.7 8.0 %collective-permute-done.3 = bf16[1024,256]{1,0:T(8,128)(2,1)} collective-permute-done((bf16[1024,256]{1,0:T(8,128)(2,1)}, bf16[1024,256]{1,0:T(8,128)(2,1)}, u32[]{:S(2)}, u32[]{:S(2)}) %collective-permute-start.3) | collective-permute-done | bytes 524320 | tf_op jit(solution)/shard_map/ppermute | solution.py:22
  100.7 1.9 bitcast_dynamic-update-slice_fusion.7
  102.6 1.9 bitcast_dynamic-update-slice_fusion.6
  104.5 1.9 bitcast_dynamic-update-slice_fusion.5
  106.4 1.9 bitcast_dynamic-update-slice_fusion.4
  108.3 1.0 bitcast_dynamic-update-slice_fusion.3
  109.3 1.9 bitcast_dynamic-update-slice_fusion.2
  111.1 1.9 bitcast_dynamic-update-slice_fusion.1
  113.9 5.0 %gather_fusion = bf16[8,1024,256]{2,1,0:T(8,128)(2,1)} fusion(bf16[8,1024,256]{2,1,0:T(8,128)(2,1)} %bitcast_dynamic-update-slice_fusion, s32[1024]{0:T(1024)S(1)} %pad_clamp_fusion), kind=kCustom, calls=%fused_computation | custom fusion | bytes 8388640 | tf_op jit(solution)/shard_map/gather | solution.py:27
  118.8 11.6 %fusion.4 = bf16[256,1024]{1,0:T(8,128)(2,1)S(1)} fusion(bf16[8192,256]{1,0:T(8,128)(2,1)} %bitcast.72, bf16[1024,8192]{1,0:T(8,128)(2,1)} %all-gather.3.cloned.1.call-done, f32[1024]{0:T(1024)S(1)} %bitcast.78), kind=kOutput, calls=%fused_computation.7 | convolution fusion | flops 4295753728 | bytes 21499904 | tf_op jit(solution)/shard_map/dot_general | solution.py:58
  130.4 1.0 fusion.7
  131.5 2.4 convolution_convert_fusion.1
  133.9 1.9 fusion.9
  135.7 110.2 %all-gather.5.cloned.1.call-done = bf16[8192,512]{0,1:T(8,128)(2,1)} async-done(((bf16[1024,512]{0,1:T(8,128)(2,1)}), bf16[8192,512]{0,1:T(8,128)(2,1)}) %all-gather.5.cloned.1.call-update) | async-done | bytes 8388624 | tf_op jit(solution)/shard_map/all_gather | solution.py:63
  246.0 15.2 %fusion.2 = bf16[1024,512]{0,1:T(8,128)(2,1)S(1)} fusion(f32[1024,512]{0,1:T(8,128)S(1)} %bitcast.67, f32[2,1024,256]{1,2,0:T(8,128)} %fusion.9, bf16[8192,512]{0,1:T(8,128)(2,1)} %all-gather.5.cloned.1.call-done, bf16[1024,8192]{1,0:T(8,128)(2,1)} %all-gather.3.cloned.1.call-done), kind=kOutput, calls=%fused_computation.4 | convolution fusion | flops 8592031744 | bytes 30408704 | tf_op jit(solution)/shard_map/dot_general | solution.py:61
  262.2 1.2 convolution_convert_fusion
  263.4 1.0 copy.20
  264.4 2.3 copy.21
  266.7 69.0 %all-reduce.3.cloned.1.call-done = (bf16[1,256,256]{2,1,0:T(8,128)(2,1)}, bf16[2,256,256]{2,1,0:T(8,128)(2,1)}, bf16[2,256,256]{2,1,0:T(8,128)(2,1)}) async-done(((bf16[1,256,256]{2,1,0:T(8,128)(2,1)}, bf16[2,256,256]{2,1,0:T(8,128)(2,1)}, bf16[2,256,256]{2,1,0:T(8,128)(2,1)}), (bf16[1,256,256]{2,1,0:T(8,128)(2,1)}, bf16[2,256,256]{2,1,0:T(8,128)(2,1)}, ...) | async-done | bytes 655376 | tf_op jit(solution)/shard_map/psum | solution.py:82
  336.7 1.5 fusion.6
  338.2 2.4 fusion.5
  (49 shorter events, 5.6 us)
Async XLA Ops:
  7.2 126.7 %copy-start = (bf16[2,256,256]{2,1,0:T(8,128)(2,1)S(1)}, bf16[2,256,256]{2,1,0:T(8,128)(2,1)}, u32[]{:S(2)}) copy-start(bf16[2,256,256]{2,1,0:T(8,128)(2,1)} %param.11) | copy-start | bytes 786436
  7.2 1.3 copy-start.5
  7.2 1.8 copy-start.11
  7.2 1.8 copy-start.12
  7.2 111.6 %all-gather.3.cloned.1.call-start = ((), (), s32[]{:S(2)}) async-start(), calls=%async_computation | async-start | bytes 20971520 | tf_op jit(solution)/shard_map/all_gather | solution.py:57
  7.9 238.0 %all-gather.5.cloned.1.call-start = ((), (), s32[]{:S(2)}) async-start(), calls=%async_computation.1 | async-start | bytes 9437184 | tf_op jit(solution)/shard_map/all_gather | solution.py:63
  10.9 97.3 %copy-start.2 = (bf16[1024,256]{1,0:T(8,128)(2,1)S(1)}, bf16[1024,256]{1,0:T(8,128)(2,1)}, u32[]{:S(2)}) copy-start(bf16[1024,256]{1,0:T(8,128)(2,1)} %param.9) | copy-start | bytes 1572868
  11.0 324.8 %all-reduce.3.cloned.1.call-start = ((), (), s32[]{:S(2)}) async-start(), calls=%async_computation.2 | async-start | bytes 1310720 | tf_op jit(solution)/shard_map/psum | solution.py:82
  12.4 18.0 %collective-permute-start = (bf16[1024,256]{1,0:T(8,128)(2,1)S(1)}, bf16[1024,256]{1,0:T(8,128)(2,1)S(1)}, u32[]{:S(2)}, u32[]{:S(2)}) collective-permute-start(bf16[1024,256]{1,0:T(8,128)(2,1)S(1)} %broadcast_multiply_fusion), channel_id=1, source_target_pairs={{0,4},{4,8},{8,12},{12,16},{16,20},{20,24},{24,28},{28,0},{1,5},{5... | collective-permute-start | bytes 1572872 | tf_op jit(solution)/shard_map/ppermute | solution.py:22
  30.3 24.6 %copy-start.7 = (bf16[1024,256]{1,0:T(8,128)(2,1)}, bf16[1024,256]{1,0:T(8,128)(2,1)S(1)}, u32[]{:S(2)}) copy-start(bf16[1024,256]{1,0:T(8,128)(2,1)S(1)} %collective-permute-done) | copy-start | bytes 1572868
  30.3 22.1 %collective-permute-start.1 = (bf16[1024,256]{1,0:T(8,128)(2,1)S(1)}, bf16[1024,256]{1,0:T(8,128)(2,1)S(1)}, u32[]{:S(2)}, u32[]{:S(2)}) collective-permute-start(bf16[1024,256]{1,0:T(8,128)(2,1)S(1)} %collective-permute-done), channel_id=1, source_target_pairs={{0,4},{4,8},{8,12},{12,16},{16,20},{20,24},{24,28},{28,0},{1,5},{5... | collective-permute-start | bytes 1572872 | tf_op jit(solution)/shard_map/ppermute | solution.py:22
  30.3 24.6 %collective-permute-start.4 = (bf16[1024,256]{1,0:T(8,128)(2,1)S(1)}, bf16[1024,256]{1,0:T(8,128)(2,1)}, u32[]{:S(2)}, u32[]{:S(2)}) collective-permute-start(bf16[1024,256]{1,0:T(8,128)(2,1)S(1)} %broadcast_multiply_fusion), channel_id=1, source_target_pairs={{4,0},{8,4},{12,8},{16,12},{20,16},{24,20},{28,24},{0,28},{5,1},{9... | collective-permute-start | bytes 1572872 | tf_op jit(solution)/shard_map/ppermute | solution.py:24
  52.5 14.7 %copy-start.8 = (bf16[1024,256]{1,0:T(8,128)(2,1)}, bf16[1024,256]{1,0:T(8,128)(2,1)S(1)}, u32[]{:S(2)}) copy-start(bf16[1024,256]{1,0:T(8,128)(2,1)S(1)} %collective-permute-done.1) | copy-start | bytes 1572868
  52.5 24.0 %collective-permute-start.2 = (bf16[1024,256]{1,0:T(8,128)(2,1)S(1)}, bf16[1024,256]{1,0:T(8,128)(2,1)}, u32[]{:S(2)}, u32[]{:S(2)}) collective-permute-start(bf16[1024,256]{1,0:T(8,128)(2,1)S(1)} %collective-permute-done.1), channel_id=1, source_target_pairs={{0,4},{4,8},{8,12},{12,16},{16,20},{20,24},{24,28},{28,0},{1,5},{5... | collective-permute-start | bytes 1572872 | tf_op jit(solution)/shard_map/ppermute | solution.py:22
  55.0 24.1 %collective-permute-start.5 = (bf16[1024,256]{1,0:T(8,128)(2,1)}, bf16[1024,256]{1,0:T(8,128)(2,1)}, u32[]{:S(2)}, u32[]{:S(2)}) collective-permute-start(bf16[1024,256]{1,0:T(8,128)(2,1)} %collective-permute-done.4), channel_id=1, source_target_pairs={{4,0},{8,4},{12,8},{16,12},{20,16},{24,20},{28,24},{0,28},{5,1},{9... | collective-permute-start | bytes 1572872 | tf_op jit(solution)/shard_map/ppermute | solution.py:24
  76.4 24.3 %collective-permute-start.3 = (bf16[1024,256]{1,0:T(8,128)(2,1)}, bf16[1024,256]{1,0:T(8,128)(2,1)}, u32[]{:S(2)}, u32[]{:S(2)}) collective-permute-start(bf16[1024,256]{1,0:T(8,128)(2,1)} %collective-permute-done.2), channel_id=1, source_target_pairs={{0,4},{4,8},{8,12},{12,16},{16,20},{20,24},{24,28},{28,0},{1,5},{5... | collective-permute-start | bytes 1572872 | tf_op jit(solution)/shard_map/ppermute | solution.py:22
  79.0 34.0 %collective-permute-start.6 = (bf16[1024,256]{1,0:T(8,128)(2,1)}, bf16[1024,256]{1,0:T(8,128)(2,1)S(1)}, u32[]{:S(2)}, u32[]{:S(2)}) collective-permute-start(bf16[1024,256]{1,0:T(8,128)(2,1)} %collective-permute-done.5), channel_id=1, source_target_pairs={{4,0},{8,4},{12,8},{16,12},{20,16},{24,20},{28,24},{0,28},{5,1},{9... | collective-permute-start | bytes 1572872 | tf_op jit(solution)/shard_map/ppermute | solution.py:24
  246.0 16.3 %copy-start.1 = (bf16[1024,512]{0,1:T(8,128)(2,1)S(1)}, bf16[1024,512]{0,1:T(8,128)(2,1)}, u32[]{:S(2)}) copy-start(bf16[1024,512]{0,1:T(8,128)(2,1)} %convert_multiply_fusion) | copy-start | bytes 3145732
  261.2 1.0 copy-start.6
  261.2 74.5 %copy-start.10 = (f32[1,256,256]{2,1,0:T(8,128)S(1)}, f32[1,256,256]{2,1,0:T(8,128)}, u32[]{:S(2)}) copy-start(f32[1,256,256]{2,1,0:T(8,128)} %param.12) | copy-start | bytes 786436
  261.2 76.9 %copy-start.9 = (f32[2,256,256]{2,1,0:T(8,128)S(1)}, f32[2,256,256]{2,1,0:T(8,128)}, u32[]{:S(2)}) copy-start(f32[2,256,256]{2,1,0:T(8,128)} %param.13) | copy-start | bytes 1572868
  336.7 3.9 %copy-start.4 = (f32[1,256,256]{2,1,0:T(8,128)}, f32[1,256,256]{2,1,0:T(8,128)S(1)}, u32[]{:S(2)}) copy-start(f32[1,256,256]{2,1,0:T(8,128)S(1)} %convert_subtract_fusion) | copy-start | bytes 786436
  338.2 2.4 copy-start.3
Sparse Core Ops, SparseCore 0:
  9.6 108.6 all-gather.2
  121.0 124.8 all-gather.4
  263.6 72.1 all-reduce.2
